TPU v7x, 128 devices: a whole 4x4x4 slice. The times are simulated.
128 devices in a mesh: dp: 16 (over y, x_hi, core), seq: 8 (over x_lo, z).
Axes of the slice: x: 4 (x_hi: 2, x_lo: 2; x = x_hi * 2 + x_lo), y: 4, z: 4, core: 2. Of those that a mesh axis runs over, the one named last changes fastest.
Arguments:
- patches: bfloat16 [16, 1024, 768], P('dp', 'seq'), may hold values from -6 to 6
- cls_tokens: bfloat16 [16, 10, 768], P('dp'), may hold values from -6 to 6
- segments: int32 [16, 1024], P('dp', 'seq'), may hold values from 0 to 10, as said below
- prompts: bfloat16 [2, 50, 768], replicated, may hold values from -6 to 6
- w_qkv: bfloat16 [2, 768, 2304], replicated, may hold values from -0.21875 to 0.21875
- w_out: bfloat16 [2, 768, 768], replicated, may hold values from -0.875 to 0.875
- w_up: bfloat16 [2, 768, 3072], replicated, may hold values from -0.21875 to 0.21875
- w_down: bfloat16 [2, 3072, 768], replicated, may hold values from -0.109375 to 0.109375
- norm_gains: float32 [2, 2, 768], replicated, may hold values from 0.5 to 1.5
- biases: float32 [2, 6, 768], replicated, may hold values from -1.5 to 1.5
- up_bias: float32 [2, 3072], replicated, may hold values from -1.5 to 1.5
- cot_patches: bfloat16 [16, 1024, 768], P('dp', 'seq'), may hold values from -6 to 6
- cot_cls: bfloat16 [16, 10, 768], P('dp'), may hold values from -6 to 6
Outputs:
- out_patches: float32 [16, 1024, 768], P('dp', 'seq')
- out_cls: float32 [16, 10, 768], P('dp')
- grad_patches: float32 [16, 1024, 768], P('dp', 'seq')
- grad_cls: float32 [16, 10, 768], P('dp')
- grad_prompts: float32 [2, 50, 768], P(None, None, ('dp', 'seq'))
- grad_qkv: float32 [2, 768, 2304], P(None, ('dp', 'seq'))
- grad_out: float32 [2, 768, 768], P(None, ('dp', 'seq'))
- grad_up: float32 [2, 768, 3072], P(None, ('dp', 'seq'))
- grad_down: float32 [2, 3072, 768], P(None, ('dp', 'seq'))
- grad_gains: float32 [2, 2, 768], P(None, None, ('dp', 'seq'))
- grad_biases: float32 [2, 6, 768], P(None, None, ('dp', 'seq'))
- grad_up_bias: float32 [2, 3072], P(None, ('dp', 'seq'))
Inputs may be any that keep to these rules, and one draw needn't show every extreme that they name: `segments`: each row holds images of one size, 100, 196 or 576 patches, numbered 0, 1, ... without gaps; slots without an image carry 10. The patches of each image, and the empty slots, are spread evenly over the row's 1024 // 128 blocks of 128 slots (counts in two blocks differ by one at most), in any order within a block.
All inputs are finite; a program needn't handle non-finite values.
Results may differ from a plain program's by a relative error of at most 0.03.
Values may be sent and summed in bfloat16 or wider, within the bound.
No kernel may reach another device: no remote copies, remote signals or barrier semaphores. Data moves between devices by JAX's collectives and lax.ppermute only.
A program may use at most 320 MiB of HBM per device.

v0:
```python
import jax
import jax.numpy as jnp
from jax import lax
from jax.sharding import PartitionSpec as P

HEADS = 12
HEAD = 64


eps_norm = 1e-06
penalty_rate = 2.0
big_negative = -1e30


def normalize(values, gain_row, shift_row):
    centre = jnp.mean(values, -1, keepdims=True)
    centred = values - centre
    spread = jnp.mean(centred * centred, -1, keepdims=True)
    return centred * lax.rsqrt(spread + eps_norm) * gain_row + shift_row


def norm_back(values, gain_row, shift_row, upstream, row_weight):
    plain = normalize(values, jnp.ones_like(gain_row), jnp.zeros_like(shift_row))
    primal, pull = jax.vjp(lambda inner: normalize(inner, gain_row, shift_row), values)
    (d_values,) = pull(upstream)
    weighted = upstream * row_weight
    lead_axes = tuple(range(values.ndim - 1))
    return (d_values, jnp.sum(weighted * plain, lead_axes), jnp.sum(weighted, lead_axes))


def project(rows_in, matrix):
    return jnp.einsum("rqd,de->rqe", rows_in, matrix, preferred_element_type=jnp.float32)


def project_back(rows_in, matrix):
    return jnp.einsum("rqe,de->rqd", rows_in, matrix, preferred_element_type=jnp.float32)


def outer_sum(left, right):
    return jnp.einsum("rqd,rqe->de", left, right, preferred_element_type=jnp.float32)


def masked_scores(query_heads, key_heads, query_segs, key_segs):
    raw = jnp.einsum(
        "qhd,khd->hqk", query_heads, key_heads, preferred_element_type=jnp.float32
    ) * HEAD ** (-0.5)
    visible = (key_segs[None, :] == query_segs[:, None]) | (key_segs[None, :] < 0)
    return (jnp.where(visible[None], raw, big_negative), visible)


def attend_forward(query_rows, key_rows, query_segs, key_segs):
    query_total, model_width = query_rows.shape
    query_heads = query_rows.reshape(query_total, HEADS, HEAD)
    key_heads = key_rows[:, :model_width].reshape(-1, HEADS, HEAD)
    value_heads = key_rows[:, model_width:].reshape(-1, HEADS, HEAD)
    scores, visible = masked_scores(query_heads, key_heads, query_segs, key_segs)
    row_top = jnp.max(scores, -1, keepdims=True)
    raised = jnp.exp(scores - row_top)
    row_total = jnp.sum(raised, -1, keepdims=True)
    weights_low = (raised / row_total).astype(jnp.bfloat16)
    attended = jnp.einsum(
        "hqk,khd->qhd", weights_low, value_heads, preferred_element_type=jnp.float32
    )
    return (
        attended.reshape(query_total, model_width).astype(jnp.bfloat16),
        row_top[..., 0] + jnp.log(row_total[..., 0]),
    )


def attend_backward(
    query_rows, key_rows, query_segs, key_segs, log_total, grad_rows, query_share, key_limit
):
    query_total, model_width = query_rows.shape
    query_heads = query_rows.reshape(query_total, HEADS, HEAD)
    key_heads = key_rows[:, :model_width].reshape(-1, HEADS, HEAD)
    value_heads = key_rows[:, model_width:].reshape(-1, HEADS, HEAD)
    scores, visible = masked_scores(query_heads, key_heads, query_segs, key_segs)
    probs_full = jnp.where(visible[None], jnp.exp(scores - log_total[..., None]), 0.0)
    grad_heads = grad_rows.reshape(query_total, HEADS, HEAD)
    d_probs = jnp.einsum(
        "qhd,khd->hqk", grad_heads, value_heads, preferred_element_type=jnp.float32
    )
    across = jnp.sum(probs_full * d_probs, -1, keepdims=True)
    d_scores = (probs_full * (d_probs - across)).astype(jnp.bfloat16)
    scale_factor = HEAD ** (-0.5)
    d_query = (
        jnp.einsum("hqk,khd->qhd", d_scores, key_heads, preferred_element_type=jnp.float32)
        * scale_factor
    )
    share_heads = query_share[None, :, None]
    d_key = (
        jnp.einsum(
            "hqk,qhd->khd", d_scores * share_heads, query_heads, preferred_element_type=jnp.float32
        )
        * scale_factor
    )
    d_value = jnp.einsum(
        "hqk,qhd->khd",
        probs_full.astype(jnp.bfloat16) * share_heads,
        grad_heads,
        preferred_element_type=jnp.float32,
    )
    return (
        d_query.reshape(query_total, model_width),
        jnp.concatenate(
            [d_key.reshape(key_limit, model_width), d_value.reshape(key_limit, model_width)], -1
        ),
        across[..., 0],
    )


def build_keys(prompt_kv, mixed, gathered, cls_count):
    row_count = mixed.shape[0]
    return jnp.concatenate(
        [prompt_kv[None], mixed[:, :cls_count, prompt_kv.shape[1] // 2 :], gathered], 1
    )


def per_device(
    patches,
    cls_tokens,
    segments,
    prompts,
    w_qkv,
    w_out,
    w_up,
    w_down,
    norm_gains,
    biases,
    up_bias,
    cot_patches,
    cot_cls,
):
    row_count, shard_len, model_width = patches.shape
    cls_count = cls_tokens.shape[1]
    prompt_count = prompts.shape[1]
    layer_count = w_qkv.shape[0]
    front_count = prompt_count + cls_count
    row_slots = shard_len * lax.axis_size("seq")
    low_type = jnp.bfloat16
    first_seq = (lax.axis_index("seq") == 0).astype(jnp.float32)
    first_all = first_seq * (lax.axis_index("dp") == 0).astype(jnp.float32)
    cls_ids = jnp.arange(cls_count, dtype=jnp.int32)
    cls_block = jnp.broadcast_to(cls_ids, (row_count, cls_count))
    query_segs = jnp.concatenate([cls_block, segments], 1)
    row_weight = jnp.concatenate(
        [jnp.full((cls_count, 1), first_seq, jnp.float32), jnp.ones((shard_len, 1), jnp.float32)], 0
    )
    row_weight_low = row_weight.astype(low_type)
    prompt_segs = jnp.full((row_count, prompt_count), -1, jnp.int32)
    tokens = jnp.concatenate([cls_tokens, patches], 1).astype(jnp.float32)
    saved = []
    for layer_at in range(layer_count):
        gain_pair = norm_gains[layer_at]
        bias_rows = biases[layer_at]
        qkv_shift = jnp.concatenate([bias_rows[1], jnp.zeros_like(bias_rows[1]), bias_rows[2]])
        prompt_full = prompts[layer_at].astype(jnp.float32)
        prompt_norm = normalize(prompt_full, gain_pair[0], bias_rows[0]).astype(low_type)
        prompt_kv = (
            jnp.dot(
                prompt_norm, w_qkv[layer_at][:, model_width:], preferred_element_type=jnp.float32
            )
            + qkv_shift[model_width:]
        ).astype(low_type)
        normed = normalize(tokens, gain_pair[0], bias_rows[0]).astype(low_type)
        mixed = (project(normed, w_qkv[layer_at]) + qkv_shift).astype(low_type)
        gathered, seg_all = (
            lax.all_gather(mixed[:, cls_count:, model_width:], "seq", axis=1, tiled=True),
            lax.all_gather(segments, "seq", axis=1, tiled=True),
        )
        key_segs = jnp.concatenate([prompt_segs, cls_block, seg_all], 1)
        key_rows = build_keys(prompt_kv, mixed, gathered, cls_count)
        attended, log_total = lax.map(
            lambda inputs_row: attend_forward(
                inputs_row[0][:, :model_width], inputs_row[1], inputs_row[2], inputs_row[3]
            ),
            (mixed, key_rows, query_segs, key_segs),
        )
        middle = tokens + (project(attended, w_out[layer_at]) + bias_rows[3])
        normed_mid = normalize(middle, gain_pair[1], bias_rows[4]).astype(low_type)
        hidden = project(normed_mid, w_up[layer_at]) + up_bias[layer_at]
        active = jax.nn.gelu(hidden, approximate=False).astype(low_type)
        kept_keys = key_rows
        saved.append(
            (
                tokens,
                normed,
                mixed,
                prompt_full,
                prompt_norm,
                prompt_kv,
                kept_keys,
                key_segs,
                attended,
                log_total,
                middle,
                normed_mid,
                hidden,
                active,
            )
        )
        tokens = middle + (project(active, w_down[layer_at]) + bias_rows[5])
    seg_first = saved[0][7][:, front_count:]
    present = (
        jnp.sum((seg_first[:, :, None] == cls_ids[None, None, :]).astype(jnp.float32), 1) > 0
    ).astype(jnp.float32)
    group_count = jnp.sum((seg_first < cls_count).astype(jnp.float32))
    count_all = lax.psum(group_count, "dp")
    valid = (segments < cls_count).astype(jnp.float32)
    upstream = jnp.concatenate(
        [
            cot_cls.astype(jnp.float32) * present[:, :, None],
            cot_patches.astype(jnp.float32) * valid[:, :, None],
        ],
        1,
    )
    layer_grads = [None] * layer_count
    for layer_at in reversed(range(layer_count)):
        (
            tokens_in,
            normed,
            mixed,
            prompt_full,
            prompt_norm,
            prompt_kv,
            kept_keys,
            key_segs,
            attended,
            log_total,
            middle,
            normed_mid,
            hidden,
            active,
        ) = saved[layer_at]
        gain_pair = norm_gains[layer_at]
        bias_rows = biases[layer_at]
        down_low = upstream.astype(low_type)
        down_weighted = down_low * row_weight_low
        layer_down = outer_sum(active, down_weighted)
        shift_down = jnp.sum(down_weighted.astype(jnp.float32), (0, 1))
        primal, gelu_pull = jax.vjp(lambda inner: jax.nn.gelu(inner, approximate=False), hidden)
        (d_hidden,) = gelu_pull(project_back(down_low, w_down[layer_at]))
        hidden_low = d_hidden.astype(low_type)
        hidden_weighted = hidden_low * row_weight_low
        layer_up = outer_sum(normed_mid, hidden_weighted)
        shift_up = jnp.sum(hidden_weighted.astype(jnp.float32), (0, 1))
        d_middle, gain_two, shift_two = norm_back(
            middle, gain_pair[1], bias_rows[4], project_back(hidden_low, w_up[layer_at]), row_weight
        )
        upstream = upstream + d_middle
        out_low = upstream.astype(low_type)
        out_weighted = out_low * row_weight_low
        layer_out = outer_sum(attended, out_weighted)
        shift_out = jnp.sum(out_weighted.astype(jnp.float32), (0, 1))
        d_attended = project_back(out_low, w_out[layer_at]).astype(low_type)
        key_rows = kept_keys
        key_limit = key_rows.shape[1]
        query_share = row_weight_low[:, 0]
        d_query, d_keys, across = lax.map(
            lambda inputs_row: attend_backward(
                inputs_row[0][:, :model_width],
                inputs_row[1],
                inputs_row[2],
                inputs_row[3],
                inputs_row[4],
                inputs_row[5],
                query_share,
                key_limit,
            ),
            (mixed, key_rows, query_segs, key_segs, log_total, d_attended),
        )
        front = lax.psum(d_keys[:, :front_count].astype(jnp.bfloat16), "seq").astype(jnp.float32)
        local_kv = lax.psum_scatter(
            d_keys[:, front_count:].astype(jnp.bfloat16), "seq", scatter_dimension=1, tiled=True
        ).astype(jnp.float32)
        mixed_grad = jnp.concatenate(
            [d_query, jnp.concatenate([front[:, prompt_count:], local_kv], 1)], 2
        ).astype(low_type)
        prompt_grad = front[:, :prompt_count].astype(low_type) * first_seq.astype(low_type)
        mixed_weighted = mixed_grad * row_weight_low
        prompt_part = jnp.einsum(
            "pd,rpe->de", prompt_norm, prompt_grad, preferred_element_type=jnp.float32
        )
        layer_qkv = outer_sum(normed, mixed_weighted) + jnp.concatenate(
            [jnp.zeros((model_width, model_width), jnp.float32), prompt_part], 1
        )
        column_sums = jnp.sum(mixed_weighted.astype(jnp.float32), (0, 1))
        prompt_sums = jnp.sum(prompt_grad.astype(jnp.float32), (0, 1))
        shift_query = column_sums[:model_width]
        shift_value = column_sums[2 * model_width :] + prompt_sums[model_width:]
        d_normed = project_back(mixed_grad, w_qkv[layer_at])
        d_tokens, gain_one, shift_one = norm_back(
            tokens_in, gain_pair[0], bias_rows[0], d_normed, row_weight
        )
        d_prompt_norm = jnp.einsum(
            "rpe,de->pd",
            prompt_grad,
            w_qkv[layer_at][:, model_width:],
            preferred_element_type=jnp.float32,
        )
        d_prompt, gain_prompt, shift_prompt = norm_back(
            prompt_full, gain_pair[0], bias_rows[0], d_prompt_norm, 1.0
        )
        upstream = upstream + d_tokens
        layer_prompt = d_prompt + penalty_rate * (count_all / row_slots) * first_all * prompt_full
        layer_gains = jnp.stack([gain_one + gain_prompt, gain_two])
        layer_biases = jnp.stack(
            [shift_one + shift_prompt, shift_query, shift_value, shift_out, shift_two, shift_down]
        )
        layer_grads[layer_at] = (
            layer_prompt,
            layer_qkv,
            layer_out,
            layer_up,
            layer_down,
            layer_gains,
            layer_biases,
            shift_up,
        )
    stacked = [jnp.stack([member[place] for member in layer_grads]) for place in range(8)]
    grad_prompts, grad_qkv, grad_out, grad_up, grad_down, grad_gains, grad_biases, grad_up_bias = (
        stacked
    )
    grad_prompts, grad_qkv, grad_out, grad_up, grad_down, grad_gains, grad_biases, grad_up_bias = (
        lax.psum_scatter(grad_prompts, ("dp", "seq"), scatter_dimension=2, tiled=True),
        lax.psum_scatter(grad_qkv, ("dp", "seq"), scatter_dimension=1, tiled=True),
        lax.psum_scatter(grad_out, ("dp", "seq"), scatter_dimension=1, tiled=True),
        lax.psum_scatter(grad_up, ("dp", "seq"), scatter_dimension=1, tiled=True),
        lax.psum_scatter(grad_down, ("dp", "seq"), scatter_dimension=1, tiled=True),
        lax.psum_scatter(grad_gains, ("dp", "seq"), scatter_dimension=2, tiled=True),
        lax.psum_scatter(grad_biases, ("dp", "seq"), scatter_dimension=2, tiled=True),
        lax.psum_scatter(grad_up_bias, ("dp", "seq"), scatter_dimension=1, tiled=True),
    )
    return (
        tokens[:, cls_count:],
        tokens[:, :cls_count],
        upstream[:, cls_count:],
        upstream[:, :cls_count],
        grad_prompts,
        grad_qkv,
        grad_out,
        grad_up,
        grad_down,
        grad_gains,
        grad_biases,
        grad_up_bias,
    )


def solution(mesh):
    placed = (
        P("dp", "seq", None),
        P("dp", None, None),
        P("dp", "seq"),
        P(),
        P(),
        P(),
        P(),
        P(),
        P(),
        P(),
        P(),
        P("dp", "seq", None),
        P("dp", None, None),
    )
    return jax.shard_map(
        per_device,
        mesh=mesh,
        in_specs=placed,
        out_specs=(
            P("dp", "seq", None),
            P("dp", None, None),
            P("dp", "seq", None),
            P("dp", None, None),
            P(None, None, ("dp", "seq")),
            P(None, ("dp", "seq"), None),
            P(None, ("dp", "seq"), None),
            P(None, ("dp", "seq"), None),
            P(None, ("dp", "seq"), None),
            P(None, None, ("dp", "seq")),
            P(None, None, ("dp", "seq")),
            P(None, ("dp", "seq")),
        ),
        check_vma=False,
    )
```

profile of v0, /device:TPU:0, one launch (start us, length us, event | category | flops | bytes accessed | tf_op | source)
XLA Modules:
  0.0 1817.6 jit_solution(15694920419628062718)
XLA Ops:
  18.4 20.0 %all_gather.11 = s32[1,1024]{1,0:T(1,128)S(1)} all-gather(s32[1,128]{1,0:T(1,128)S(1)} %copy-done.178), channel_id=1, replica_groups=mesh['dp'=16,'seq'=8] {'seq'}, dimensions={1}, use_global_device_ids=true | all-gather | bytes 4608 | tf_op jit(solution)/shard_map/all_gather | solution.py:169
  49.2 14.5 all-gather.3.cloned.1.call-done
  63.7 16.5 concatenate.178
  98.6 6.0 multiply_convert_fusion.3
  114.9 37.5 %all-gather.5.cloned.1.call-done = bf16[1,1024,1536]{2,1,0:T(8,128)(2,1)} async-done(((bf16[1,128,1536]{2,1,0:T(8,128)(2,1)}), bf16[1,1024,1536]{2,1,0:T(8,128)(2,1)}) %all-gather.5.cloned.1.call-update) | async-done | bytes 3145744 | tf_op jit(solution)/shard_map/all_gather | solution.py:168
  152.4 18.5 %concatenate.186 = bf16[1,1084,1536]{2,1,0:T(8,128)(2,1)} concatenate(bf16[1,50,1536]{2,1,0:T(8,128)(2,1)S(1)} %fusion.56, bf16[1,10,1536]{2,1,0:T(8,128)(2,1)S(1)} %slice.331, bf16[1,1024,1536]{2,1,0:T(8,128)(2,1)} %all-gather.5.cloned.1.call-done), dimensions={1} | concatenate | bytes 6660096 | tf_op jit(solution)/shard_map/concatenate | solution.py:114
  209.8 7.4 multiply_reduce_fusion.1
  237.7 15.8 copy.102
  264.7 42.0 %all-reduce.20.cloned.1.call-done = bf16[1,60,1536]{1,2,0:T(8,128)(2,1)} async-done(((bf16[1,60,1536]{1,2,0:T(8,128)(2,1)}), bf16[1,60,1536]{1,2,0:T(8,128)(2,1)}) %all-reduce.20.cloned.1.call-update) | async-done | bytes 184336 | tf_op jit(solution)/shard_map/psum | solution.py:272
  307.9 46.7 %reduce-scatter.12.cloned.1.call-done = bf16[128,1536]{1,0:T(8,128)(2,1)} async-done(((bf16[1024,1536]{1,0:T(8,128)(2,1)}), bf16[128,1536]{1,0:T(8,128)(2,1)}) %reduce-scatter.12.cloned.1.call-update) | async-done | bytes 393232
  376.4 6.8 multiply_reduce_fusion
  404.0 15.8 copy.104
  428.8 6.5 convolution_bitcast_fusion.2
  450.6 22.4 %all-reduce.22.cloned.1.call-done = bf16[1,60,1536]{1,2,0:T(8,128)(2,1)} async-done(((bf16[1,60,1536]{1,2,0:T(8,128)(2,1)}), bf16[1,60,1536]{1,2,0:T(8,128)(2,1)}) %all-reduce.22.cloned.1.call-update) | async-done | bytes 184336 | tf_op jit(solution)/shard_map/psum | solution.py:272
  478.9 41.9 %reduce-scatter.14.cloned.1.call-done = bf16[128,1536]{1,0:T(8,128)(2,1)} async-done(((bf16[1024,1536]{1,0:T(8,128)(2,1)}), bf16[128,1536]{1,0:T(8,128)(2,1)}) %reduce-scatter.14.cloned.1.call-update) | async-done | bytes 393232
  537.5 7.1 pad_maximum_fusion
  544.6 37.0 %copy.97 = f32[2,768,3072]{2,0,1:T(2,128)} copy(f32[2,768,3072]{2,1,0:T(8,128)S(1)} %pad_maximum_fusion) | data formatting | bytes 37748736 | tf_op jit(solution)/shard_map/stack | solution.py:320
  582.9 34.7 %psum.23 = f32[]{:T(128)} all-reduce(f32[]{:T(128)} %fusion.225), channel_id=1, replica_groups=mesh['dp'=16,'seq'=8] {'dp'}, use_global_device_ids=true, to_apply=%region_34.35 | all-reduce | flops 1 | bytes 8 | tf_op jit(solution)/shard_map/psum | solution.py:208
  637.8 11.0 pad_maximum_fusion.2
  648.8 26.9 %copy.95 = f32[2,768,2304]{2,0,1:T(2,128)} copy(f32[2,768,2304]{2,1,0:T(8,128)} %pad_maximum_fusion.2) | data formatting | bytes 28311552 | tf_op jit(solution)/shard_map/stack | solution.py:320
  680.1 6.6 pad_maximum_fusion.1
  697.8 211.5 %all-reduce.24.cloned.1.call-done = f32[2,768,3072]{2,0,1:T(2,128)} async-done(((f32[2,768,3072]{2,0,1:T(2,128)}), f32[2,768,3072]{2,0,1:T(2,128)}) %all-reduce.24.cloned.1.call-update) | async-done | bytes 18874384
  910.9 225.6 %all-reduce.28.cloned.1.call-done = (f32[2,50,768]{1,0,2:T(2,128)}, f32[2,768,2304]{2,0,1:T(2,128)}, f32[2,768,768]{2,0,1:T(2,128)}) async-done(((f32[2,50,768]{1,0,2:T(2,128)}, f32[2,768,2304]{2,0,1:T(2,128)}, f32[2,768,768]{2,0,1:T(2,128)}), (f32[2,50,768]{1,0,2:T(2,128)}, f32[2,768,2304]{2,0,1:T(2,128)}, f32[2,768,768]{2,0,1:T(2,128)})) %all-reduce.28.cloned.1.call-update) | async-done | bytes 19181584
  1140.8 669.8 %reduce-scatter.10.cloned.1.call-done = f32[2,24,768]{2,1,0:T(8,128)} async-done(((f32[2,3072,768]{2,1,0:T(8,128)}), f32[2,24,768]{2,1,0:T(8,128)}) %reduce-scatter.10.cloned.1.call-update) | async-done | bytes 147472 | tf_op jit(solution)/shard_map/reduce_scatter | solution.py:329
  (640 shorter events, 251.3 us)
Async XLA Ops:
  7.2 56.6 %all-gather.3.cloned.1.call-start = ((), (), s32[]{:S(2)}) async-start(), calls=%async_computation.3 | async-start | bytes 3538944 | tf_op jit(solution)/shard_map/all_gather | solution.py:168
  8.8 37.7 %copy-start.89 = (f32[768]{0:T(1024)}, f32[768]{0:T(1024)S(1)}, u32[]{:S(2)}) copy-start(f32[768]{0:T(1024)S(1)} %get-tuple-element.192) | copy-start | bytes 9220
  8.8 103.0 %copy-start.100 = (f32[768]{0:T(1024)}, f32[768]{0:T(1024)S(1)}, u32[]{:S(2)}) copy-start(f32[768]{0:T(1024)S(1)} %get-tuple-element.186) | copy-start | bytes 9220
  16.7 135.7 %all-gather.5.cloned.1.call-start = ((), (), s32[]{:S(2)}) async-start(), calls=%async_computation.4 | async-start | bytes 3538944 | tf_op jit(solution)/shard_map/all_gather | solution.py:168
  38.4 71.3 %copy-start.92 = (s32[1,1024]{1,0:T(1,128)}, s32[1,1024]{1,0:T(1,128)S(1)}, u32[]{:S(2)}) copy-start(s32[1,1024]{1,0:T(1,128)S(1)} %all_gather.11) | copy-start | bytes 12292
  48.6 40.2 %copy-start.11 = (pred[138,1084]{1,0:T(8,128)(4,1)}, pred[138,1084]{1,0:T(8,128)(4,1)S(1)}, u32[]{:S(2)}) copy-start(pred[138,1084]{1,0:T(8,128)(4,1)S(1)} %compare_or_fusion) | copy-start | bytes 448780
  108.3 198.4 %all-reduce.20.cloned.1.call-start = ((), (), s32[]{:S(2)}) async-start(), calls=%async_computation.5 | async-start | bytes 786432 | tf_op jit(solution)/shard_map/psum | solution.py:272
  232.3 122.4 %reduce-scatter.12.cloned.1.call-start = ((), (), s32[]{:S(2)}) async-start(), calls=%async_computation.8 | async-start | bytes 3538944
  258.9 214.2 %all-reduce.22.cloned.1.call-start = ((), (), s32[]{:S(2)}) async-start(), calls=%async_computation.6 | async-start | bytes 786432 | tf_op jit(solution)/shard_map/psum | solution.py:272
  307.9 51.9 %copy-start.35 = (bf16[1,10,1536]{1,2,0:T(8,128)(2,1)}, bf16[1,10,1536]{1,2,0:T(8,128)(2,1)S(1)}, u32[]{:S(2)}) copy-start(bf16[1,10,1536]{1,2,0:T(8,128)(2,1)S(1)} %slice.339) | copy-start | bytes 92164
  307.9 51.9 %copy-start.17 = (f32[138,768]{1,0:T(8,128)S(1)}, f32[138,768]{1,0:T(8,128)}, u32[]{:S(2)}) copy-start(f32[138,768]{1,0:T(8,128)} %copy-done.15) | copy-start | bytes 1271812
  307.9 51.9 %copy-start.28 = (bf16[12,64,138]{2,1,0:T(8,128)(2,1)S(1)}, bf16[12,64,138]{2,1,0:T(8,128)(2,1)}, u32[]{:S(2)}) copy-start(bf16[12,64,138]{2,1,0:T(8,128)(2,1)} %fusion.86) | copy-start | bytes 635908
  307.9 51.9 %copy-start.120 = (f32[138]{0:T(256)S(1)}, f32[138]{0:T(256)}, u32[]{:S(2)}) copy-start(f32[138]{0:T(256)} %copy-done.119) | copy-start | bytes 1660
  307.9 51.9 %copy-start.148 = (f32[138]{0:T(256)S(1)}, f32[138]{0:T(256)}, u32[]{:S(2)}) copy-start(f32[138]{0:T(256)} %copy-done.147) | copy-start | bytes 1660
  307.9 51.9 %copy-start.163 = (f32[138]{0:T(256)S(1)}, f32[138]{0:T(256)}, u32[]{:S(2)}) copy-start(f32[138]{0:T(256)} %concatenate.191) | copy-start | bytes 1660
  398.5 122.3 %reduce-scatter.14.cloned.1.call-start = ((), (), s32[]{:S(2)}) async-start(), calls=%async_computation.9 | async-start | bytes 3538944
  425.1 268.8 %all-reduce.26.cloned.1.call-start = ((), (), s32[]{:S(2)}) async-start(), calls=%async_computation.11 | async-start | bytes 1646592
  477.8 50.1 %copy-start.176 = (f32[50]{0:T(128)}, f32[50]{0:T(128)S(1)}, u32[]{:S(2)}) copy-start(f32[50]{0:T(128)S(1)} %multiply_multiply_fusion.15) | copy-start | bytes 604
  478.8 49.0 %copy-start.29 = (bf16[12,64,138]{2,1,0:T(8,128)(2,1)S(1)}, bf16[12,64,138]{2,1,0:T(8,128)(2,1)}, u32[]{:S(2)}) copy-start(bf16[12,64,138]{2,1,0:T(8,128)(2,1)} %fusion.86) | copy-start | bytes 635908
  478.9 49.0 %copy-start.31 = (bf16[12,64,138]{2,1,0:T(8,128)(2,1)S(1)}, bf16[12,64,138]{2,1,0:T(8,128)(2,1)}, u32[]{:S(2)}) copy-start(bf16[12,64,138]{2,1,0:T(8,128)(2,1)} %fusion.87) | copy-start | bytes 635908
  478.9 49.0 %copy-start.36 = (bf16[1,10,1536]{1,2,0:T(8,128)(2,1)S(1)}, bf16[1,10,1536]{1,2,0:T(8,128)(2,1)}, u32[]{:S(2)}) copy-start(bf16[1,10,1536]{1,2,0:T(8,128)(2,1)} %copy-done.35) | copy-start | bytes 92164
  537.5 371.9 %all-reduce.24.cloned.1.call-start = ((), (), s32[]{:S(2)}) async-start(), calls=%async_computation.10 | async-start | bytes 37748736
  581.8 554.8 %all-reduce.28.cloned.1.call-start = ((), (), s32[]{:S(2)}) async-start(), calls=%async_computation.12 | async-start | bytes 39321600
  675.8 1134.8 %reduce-scatter.10.cloned.1.call-start = ((), (), s32[]{:S(2)}) async-start(), calls=%async_computation.7 | async-start | bytes 19021824 | tf_op jit(solution)/shard_map/reduce_scatter | solution.py:329
  (192 other events, 1222.5 us)
Sparse Core Ops, SparseCore 0:
  16.9 46.8 all-gather.2
  108.4 43.9 all-gather.4
  232.4 74.2 all-reduce.19
  309.1 45.5 reduce-scatter.11
  398.6 74.3 all-reduce.21
  475.3 45.4 reduce-scatter.13
  537.6 145.9 all-reduce.25
  689.8 219.5 all-reduce.23
  915.6 220.8 all-reduce.27
  1139.3 671.1 reduce-scatter.9
where the time goes:
time: 1830 us; the launch traced here: 1820 us
  waiting for transfers between devices  1310 us (72%)
  local copies, waits for them, and re-layouts  248 us (14%)
  matrix products  122 us (7%)
  other arithmetic  62 us (3%)
  blocking collectives  54.7 us (3%)
    reduce_scatter x1, waiting for transfers between devices, per_device(): lax.psum_scatter(grad_down, ('dp', 'seq'), scatter_dimension=1, tiled=True)  670 us
    unnamed x15, waiting for transfers between devices  526 us
    unnamed x430, local copies, waits for them, and re-layouts  82.1 us
    another operation x5, local copies, waits for them, and re-layouts, per_device(): jnp.stack([member[place] for member in layer_grads])  72.1 us
    psum x2, waiting for transfers between devices, per_device(): lax.psum(d_keys[:, :front_count].astype(jnp.bfloat16), 'seq')  64.4 us
    all_gather x2, waiting for transfers between devices, per_device(): lax.all_gather(mixed[:, cls_count:, model_width:], 'seq', axis=1, tiled=T...  52 us
  transfers between devices with their start and end apart: 10, of which 9 were waited for; matrix products, arithmetic and copies ran while one was open for 13% of the time, Pallas kernels for 0%

commit v1 on v0

--- a/solution.py
+++ b/solution.py
@@ -10,6 +10,64 @@
 eps_norm = 1e-06
 penalty_rate = 2.0
 big_negative = -1e30
+
+AXES = ("dp", "seq")
+
+
+def place_of(device):
+    dp, seq = device // 8, device % 8
+    return {"core": dp % 2, "x": dp // 2 % 2 * 2 + seq // 4, "y": dp // 4, "z": seq % 4}
+
+
+def device_of(place):
+    dp = (place["y"] * 2 + place["x"] // 2) * 2 + place["core"]
+    return dp * 8 + place["x"] % 2 * 4 + place["z"]
+
+
+SPAN = {"core": 2, "x": 4, "y": 4, "z": 4}
+
+
+def moved(axis, step):
+    pairs = []
+    for device in range(128):
+        place = place_of(device)
+        place[axis] = (place[axis] + step) % SPAN[axis]
+        pairs.append((device, device_of(place)))
+    return pairs
+
+
+def send(values, axis, step):
+    return lax.ppermute(values, AXES, moved(axis, step))
+
+
+def owner_order(axes):
+    here = place_of(lax.axis_index("dp") * 8 + lax.axis_index("seq"))
+    total = 1
+    for axis in axes:
+        total *= SPAN[axis]
+    rest = jnp.arange(total, dtype=jnp.int32)
+    place = {}
+    for axis in reversed(axes):
+        place[axis] = (here[axis] + rest % SPAN[axis]) % SPAN[axis]
+        rest = rest // SPAN[axis]
+    return device_of(place)
+
+
+def ring_sum(pieces, axis):
+    total = pieces[0].astype(jnp.float32)
+    for step in range(1, SPAN[axis]):
+        total = total + send(pieces[step], axis, step).astype(jnp.float32)
+    return total
+
+
+def fold(values, axis):
+    return ring_sum(jnp.split(values, SPAN[axis], 0), axis)
+
+
+def fold_second(values, first, axis):
+    blocks = values.reshape(SPAN[first], SPAN[axis], -1, values.shape[1])
+    pieces = [blocks[:, step].reshape(-1, values.shape[1]) for step in range(SPAN[axis])]
+    return ring_sum(pieces, axis)
 
 
 def normalize(values, gain_row, shift_row):
@@ -317,20 +375,64 @@
             layer_biases,
             shift_up,
         )
-    stacked = [jnp.stack([member[place] for member in layer_grads]) for place in range(8)]
-    grad_prompts, grad_qkv, grad_out, grad_up, grad_down, grad_gains, grad_biases, grad_up_bias = (
-        stacked
-    )
-    grad_prompts, grad_qkv, grad_out, grad_up, grad_down, grad_gains, grad_biases, grad_up_bias = (
-        lax.psum_scatter(grad_prompts, ("dp", "seq"), scatter_dimension=2, tiled=True),
-        lax.psum_scatter(grad_qkv, ("dp", "seq"), scatter_dimension=1, tiled=True),
-        lax.psum_scatter(grad_out, ("dp", "seq"), scatter_dimension=1, tiled=True),
-        lax.psum_scatter(grad_up, ("dp", "seq"), scatter_dimension=1, tiled=True),
-        lax.psum_scatter(grad_down, ("dp", "seq"), scatter_dimension=1, tiled=True),
-        lax.psum_scatter(grad_gains, ("dp", "seq"), scatter_dimension=2, tiled=True),
-        lax.psum_scatter(grad_biases, ("dp", "seq"), scatter_dimension=2, tiled=True),
-        lax.psum_scatter(grad_up_bias, ("dp", "seq"), scatter_dimension=1, tiled=True),
-    )
+    low = low_type
+    order = owner_order(("core", "z", "x", "y"))
+    rows_wanted = (order[:, None] * 6 + jnp.arange(6, dtype=jnp.int32)).reshape(-1)
+    picker = (rows_wanted[:, None] == jnp.arange(model_width, dtype=jnp.int32)[None, :]).astype(low)
+
+    def picked(grad):
+        return jnp.dot(picker, grad.astype(low), preferred_element_type=jnp.float32).astype(low)
+
+    grads_of = lambda place: [member[place] for member in layer_grads]
+    small = jnp.concatenate(
+        [member for member in grads_of(0)]
+        + grads_of(5)
+        + grads_of(6)
+        + [member.reshape(model_width, 4).T for member in grads_of(7)]
+        + [jnp.zeros((4, model_width), jnp.float32)],
+        0,
+    )
+    group_up = picked(jnp.concatenate(grads_of(3), 1))
+    group_mixed = picked(jnp.concatenate(grads_of(1) + grads_of(2) + [small.T], 1))
+    down_order = owner_order(("core", "y", "z", "x"))
+    group_down = jnp.concatenate(
+        [
+            jnp.take(member.astype(low).reshape(128, 24, model_width), down_order, 0).reshape(
+                -1, model_width
+            )
+            for member in grads_of(4)
+        ],
+        1,
+    )
+    group_up = fold(group_up, "core").astype(low)
+    group_down = fold(group_down, "core").astype(low)
+    group_mixed = fold(group_mixed, "core").astype(low)
+    group_up = fold(group_up, "z").astype(low)
+    group_down = fold(group_down, "y").astype(low)
+    group_mixed = fold_second(group_mixed, "z", "x").astype(low)
+    group_up = fold(group_up, "x").astype(low)
+    group_down = fold(group_down, "z").astype(low)
+    group_mixed = fold(group_mixed, "z").astype(low)
+    group_up = fold(group_up, "y")
+    group_down = fold(group_down, "x")
+    group_mixed = fold(group_mixed, "y")
+
+    def columns(group, edges):
+        out, at = [], 0
+        for width in edges:
+            out.append(group[:, at : at + width])
+            at += width
+        return out
+
+    grad_up = jnp.stack(columns(group_up, [3072] * 2))
+    grad_down = jnp.stack(columns(group_down, [768] * 2))
+    mixed_parts = columns(group_mixed, [2304] * 2 + [768] * 2 + [50, 50, 2, 2, 6, 6, 4, 4])
+    grad_qkv = jnp.stack(mixed_parts[:2])
+    grad_out = jnp.stack(mixed_parts[2:4])
+    grad_prompts = jnp.stack([part.T for part in mixed_parts[4:6]])
+    grad_gains = jnp.stack([part.T for part in mixed_parts[6:8]])
+    grad_biases = jnp.stack([part.T for part in mixed_parts[8:10]])
+    grad_up_bias = jnp.stack([part.reshape(-1) for part in mixed_parts[10:12]])
     return (
         tokens[:, cls_count:],
         tokens[:, :cls_count],

time: 1830 us -> 769 us (0.42)
  waiting for transfers between devices: 1310 us -> 218 us
  local copies, waits for them, and re-layouts: 248 us -> 201 us
  starting transfers between devices: 0.59 us -> 41 us
  matrix products: 122 us -> 148 us
    reduce_scatter x1 -> x0, waiting for transfers between devices: 670 us -> none  [per_device(): lax.psum_scatter(grad_down, ('dp', 'seq'), scatter_dimension=1, tiled=True)]
    unnamed x15 -> x8, waiting for transfers between devices: 526 us -> 20.5 us
    ppermute x0 -> x30, waiting for transfers between devices: none -> 124 us  [send(): return lax.ppermute(values, AXES, moved(axis, step))]
    another operation x6 -> x8, local copies, waits for them, and re-layouts: 72.1 us -> 0.27 us  [the longest x2 0.15 us: per_device(): grad_up_bias = jnp.stack([part.reshape(-1) for part in mixed_parts[10:12]])]
    psum x2, waiting for transfers between devices: 64.4 us -> 23 us  [per_device(): lax.psum(d_keys[:, :front_count].astype(jnp.bfloat16), 'seq')]
    ppermute x0 -> x30, starting transfers between devices: none -> 40.4 us  [send(): return lax.ppermute(values, AXES, moved(axis, step))]
    another operation x16 -> x20, other arithmetic: 29.5 us -> 5.84 us  [the longest x12 27.3 us: per_device(): jnp.stack([member[place] for member in layer_grads])]
    dot_general x0 -> x2, matrix products: none -> 22.4 us  [picked(): jnp.dot(picker, grad.astype(low), preferred_element_type=jnp.float32)]
  transfers between devices with their start and end apart: 10 -> 36, of which waited for: 9 -> 15; matrix products, arithmetic and copies ran while one was open for 13% -> 29% of each run, Pallas kernels for 0% -> 0%
where the time goes in v1:
time: 769 us; the launch traced here: 761 us
  waiting for transfers between devices  218 us (28%)
  local copies, waits for them, and re-layouts  201 us (26%)
  matrix products  148 us (19%)
  other arithmetic  79.4 us (10%)
  blocking collectives  55.7 us (7%)
  starting transfers between devices  41 us (5%)
  between operations  17.5 us (2%)
    ppermute x30, waiting for transfers between devices, send(): return lax.ppermute(values, AXES, moved(axis, step))  124 us
    unnamed x391, local copies, waits for them, and re-layouts  72.7 us
    all_gather x2, waiting for transfers between devices, per_device(): lax.all_gather(mixed[:, cls_count:, model_width:], 'seq', axis=1, tiled=T...  50.5 us
    ppermute x30, starting transfers between devices, send(): return lax.ppermute(values, AXES, moved(axis, step))  40.4 us
    psum x1, blocking collectives, per_device(): count_all = lax.psum(group_count, 'dp')  35.7 us
    concatenate x2, local copies, waits for them, and re-layouts, build_keys(): jnp.concatenate([prompt_kv[None], mixed[:, :cls_count, prompt_kv.shape[1]...  32.9 us
    psum x2, waiting for transfers between devices, per_device(): lax.psum(d_keys[:, :front_count].astype(jnp.bfloat16), 'seq')  23 us
    dot_general x8, matrix products, project(): jnp.einsum('rqd,de->rqe', rows_in, matrix, preferred_element_type=jnp.flo...  22.7 us
  transfers between devices with their start and end apart: 36, of which 15 were waited for; matrix products, arithmetic and copies ran while one was open for 29% of the time, Pallas kernels for 0%

profile of v1, /device:TPU:0, one launch (start us, length us, event | category | flops | bytes accessed | tf_op | source)
XLA Modules:
  0.0 760.9 jit_solution(532470559744558819)
XLA Ops:
  19.6 20.0 %all_gather.11 = s32[1,1024]{1,0:T(1,128)S(1)} all-gather(s32[1,128]{1,0:T(1,128)S(1)} %copy-done.152), channel_id=1, replica_groups=mesh['dp'=16,'seq'=8] {'seq'}, dimensions={1}, use_global_device_ids=true | all-gather | bytes 4608 | tf_op jit(solution)/shard_map/all_gather | solution.py:227
  48.9 15.0 %all-gather.3.cloned.1.call-done = bf16[1,1024,1536]{2,1,0:T(8,128)(2,1)} async-done(((bf16[1,128,1536]{2,1,0:T(8,128)(2,1)}), bf16[1,1024,1536]{2,1,0:T(8,128)(2,1)}) %all-gather.3.cloned.1.call-update) | async-done | bytes 3145744 | tf_op jit(solution)/shard_map/all_gather | solution.py:226
  63.9 16.5 %concatenate.193 = bf16[1,1084,1536]{2,1,0:T(8,128)(2,1)S(1)} concatenate(bf16[1,50,1536]{2,1,0:T(8,128)(2,1)} %fusion.66, bf16[1,10,1536]{2,1,0:T(8,128)(2,1)} %slice.411, bf16[1,1024,1536]{2,1,0:T(8,128)(2,1)} %all-gather.3.cloned.1.call-done), dimensions={1} | concatenate | bytes 6660096 | tf_op jit(solution)/shard_map/concatenate | solution.py:172
  98.1 7.9 %multiply_convert_fusion.3 = (bf16[138,3072]{1,0:T(8,128)(2,1)S(1)}, f32[138,3072]{1,0:T(8,128)}, f32[138,3072]{1,0:T(8,128)}) fusion(f32[3072]{0:T(1024)S(1)} %bitcast.426, bf16[2,768,3072]{2,1,0:T(8,128)(2,1)} %param.21, f32[138,768]{1,0:T(8,128)S(1)} %get-tuple-element.292, f32[768]{0:T(1024)S(1)} %get-tuple-element.197, ...), kind=kOutput, calls=%fused_computation.138 | convolution fusion | flops 679675392 | bytes 9401424 | tf_op jit(solution)/shard_map/rqd,de->rqe/dot_general | solution.py:90
  117.8 35.5 %all-gather.5.cloned.1.call-done = bf16[1,1024,1536]{2,1,0:T(8,128)(2,1)} async-done(((bf16[1,128,1536]{2,1,0:T(8,128)(2,1)}), bf16[1,1024,1536]{2,1,0:T(8,128)(2,1)}) %all-gather.5.cloned.1.call-update) | async-done | bytes 3145744 | tf_op jit(solution)/shard_map/all_gather | solution.py:226
  153.3 16.5 %concatenate.201 = bf16[1,1084,1536]{2,1,0:T(8,128)(2,1)S(1)} concatenate(bf16[1,50,1536]{2,1,0:T(8,128)(2,1)} %fusion.65, bf16[1,10,1536]{2,1,0:T(8,128)(2,1)} %slice.417, bf16[1,1024,1536]{2,1,0:T(8,128)(2,1)} %all-gather.5.cloned.1.call-done), dimensions={1} | concatenate | bytes 6660096 | tf_op jit(solution)/shard_map/concatenate | solution.py:172
  204.1 7.0 multiply_reduce_fusion.1
  231.6 15.9 %copy.212 = bf16[1,1024,1536]{2,0,1:T(2,128)(2,1)} copy(bf16[1,1024,1536]{1,2,0:T(8,128)(2,1)} %slice.426) | data formatting | bytes 6291456
  254.1 35.7 %psum.23 = f32[]{:T(128)} all-reduce(f32[]{:T(128)} %fusion.239), channel_id=1, replica_groups=mesh['dp'=16,'seq'=8] {'dp'}, use_global_device_ids=true, to_apply=%region_34.35 | all-reduce | flops 1 | bytes 8 | tf_op jit(solution)/shard_map/psum | solution.py:266
  327.9 20.4 %reduce-scatter.7.cloned.1.call-done = bf16[128,1536]{1,0:T(8,128)(2,1)} async-done(((bf16[1024,1536]{1,0:T(8,128)(2,1)}), bf16[128,1536]{1,0:T(8,128)(2,1)}) %reduce-scatter.7.cloned.1.call-update) | async-done | bytes 393232
  367.6 6.1 multiply_reduce_fusion
  373.8 7.0 fusion.35
  384.4 13.7 %multiply_convert_fusion = bf16[12,138,1084]{2,1,0:T(8,128)(2,1)S(1)} fusion(f32[12,138,1084]{2,1,0:T(8,128)S(1)} %get-tuple-element.307, f32[12,138,1084]{2,1,0:T(8,128)S(1)} %bitcast.346, f32[12,138]{1,0:T(8,128)S(1)} %get-tuple-element.306, f32[12,138]{1,0:T(8,128)S(1)} %copy-done.78, pred[138,1084]{1,0:T(8,128)(4,1)S(1)} %copy-done.16), kind=kLoop, calls=%fused_computation.12 | loop fusion | flops 8975520 | bytes 18113880 | tf_op jit(solution)/shard_map/while/body/eval_jaxpr/convert_element_type | solution.py:142
  406.1 6.9 broadcast_select_fusion.1
  423.4 15.8 %copy.214 = bf16[1,1024,1536]{2,0,1:T(2,128)(2,1)} copy(bf16[1,1024,1536]{1,2,0:T(8,128)(2,1)} %slice.429) | data formatting | bytes 6291456
  446.4 10.4 %convolution_convert_fusion.1 = bf16[768,6144]{1,0:T(8,128)(2,1)} fusion(bf16[768,3072]{1,0:T(8,128)(2,1)S(1)} %bitcast.363, bf16[768,3072]{1,0:T(8,128)(2,1)S(1)} %convolution_convert_fusion.5, s32[768]{0:T(1024)S(1)} %copy-done.138), kind=kOutput, calls=%fused_computation.3 | convolution fusion | flops 7271940096 | bytes 18877440 | tf_op jit(solution)/shard_map/dot_general | solution.py:384
  475.1 23.0 %all-reduce.10.cloned.1.call-done = bf16[1,60,1536]{1,2,0:T(8,128)(2,1)} async-done(((bf16[1,60,1536]{1,2,0:T(8,128)(2,1)}), bf16[1,60,1536]{1,2,0:T(8,128)(2,1)}) %all-reduce.10.cloned.1.call-update) | async-done | bytes 184336 | tf_op jit(solution)/shard_map/psum | solution.py:330
  506.6 6.0 add_convert_fusion.1
  526.9 17.1 %collective-permute-done.21 = bf16[384,1536]{1,0:T(8,128)(2,1)} collective-permute-done((bf16[384,1536]{1,0:T(8,128)(2,1)}, bf16[384,1536]{1,0:T(8,128)(2,1)}, u32[]{:S(2)}, u32[]{:S(2)}) %collective-permute-start.21) | collective-permute-done | bytes 1179680 | tf_op jit(solution)/shard_map/ppermute | solution.py:40
  546.9 17.8 %collective-permute-done.22 = bf16[384,1536]{1,0:T(8,128)(2,1)} collective-permute-done((bf16[384,1536]{1,0:T(8,128)(2,1)}, bf16[384,1536]{1,0:T(8,128)(2,1)}, u32[]{:S(2)}, u32[]{:S(2)}) %collective-permute-start.22) | collective-permute-done | bytes 1179680 | tf_op jit(solution)/shard_map/ppermute | solution.py:40
  570.5 23.0 %collective-permute-done.11 = bf16[96,6144]{1,0:T(8,128)(2,1)S(1)} collective-permute-done((bf16[96,6144]{1,0:T(8,128)(2,1)S(1)}, bf16[96,6144]{1,0:T(8,128)(2,1)S(1)}, u32[]{:S(2)}, u32[]{:S(2)}) %collective-permute-start.11) | collective-permute-done | bytes 1179680 | tf_op jit(solution)/shard_map/ppermute | solution.py:40
  637.4 12.1 %convolution_convert_fusion = bf16[768,6272]{1,0:T(8,128)(2,1)S(1)} fusion(bf16[768,6272]{1,0:T(8,128)(2,1)} %bitcast_dynamic-update-slice_fusion, s32[768]{0:T(1024)S(1)} %copy-done.138), kind=kOutput, calls=%fused_computation.2 | convolution fusion | flops 7404158976 | bytes 19270656 | tf_op jit(solution)/shard_map/dot_general | solution.py:384
  673.2 50.7 %collective-permute-done.29 = bf16[24,1536]{1,0:T(8,128)(2,1)S(1)} collective-permute-done((bf16[24,1536]{1,0:T(8,128)(2,1)S(1)}, bf16[24,1536]{1,0:T(8,128)(2,1)S(1)}, u32[]{:S(2)}, u32[]{:S(2)}) %collective-permute-start.29) | collective-permute-done | bytes 73760 | tf_op jit(solution)/shard_map/ppermute | solution.py:40
  730.3 10.2 %collective-permute-done.4 = bf16[24,6272]{1,0:T(8,128)(2,1)S(1)} collective-permute-done((bf16[24,6272]{1,0:T(8,128)(2,1)S(1)}, bf16[24,6272]{1,0:T(8,128)(2,1)S(1)}, u32[]{:S(2)}, u32[]{:S(2)}) %collective-permute-start.4) | collective-permute-done | bytes 301088 | tf_op jit(solution)/shard_map/ppermute | solution.py:40
  (702 shorter events, 333.3 us)
Async XLA Ops:
  7.2 56.7 %all-gather.3.cloned.1.call-start = ((), (), s32[]{:S(2)}) async-start(), calls=%async_computation.2 | async-start | bytes 3538944 | tf_op jit(solution)/shard_map/all_gather | solution.py:226
  16.8 136.5 %all-gather.5.cloned.1.call-start = ((), (), s32[]{:S(2)}) async-start(), calls=%async_computation.3 | async-start | bytes 3538944 | tf_op jit(solution)/shard_map/all_gather | solution.py:226
  109.2 211.1 %all-reduce.8.cloned.1.call-start = ((), (), s32[]{:S(2)}) async-start(), calls=%async_computation.4 | async-start | bytes 786432 | tf_op jit(solution)/shard_map/psum | solution.py:330
  226.2 122.1 %reduce-scatter.7.cloned.1.call-start = ((), (), s32[]{:S(2)}) async-start(), calls=%async_computation.6 | async-start | bytes 3538944
  252.8 245.3 %all-reduce.10.cloned.1.call-start = ((), (), s32[]{:S(2)}) async-start(), calls=%async_computation.5 | async-start | bytes 786432 | tf_op jit(solution)/shard_map/psum | solution.py:330
  418.9 87.7 %collective-permute-start.20 = (bf16[1536,1536]{1,0:T(8,128)(2,1)}, bf16[1536,1536]{1,0:T(8,128)(2,1)}, u32[]{:S(2)}, u32[]{:S(2)}) collective-permute-start(bf16[1536,1536]{1,0:T(8,128)(2,1)} %pad_maximum_fusion), channel_id=1, source_target_pairs={{0,8},{1,9},{2,10},{3,11},{4,12},{5,13},{6,14},{7,15},{8,0},{9,1},... | collective-permute-start | bytes 14155784 | tf_op jit(solution)/shard_map/ppermute | solution.py:40
  423.3 179.9 %reduce-scatter.9.cloned.1.call-start = ((), (), s32[]{:S(2)}) async-start(), calls=%async_computation.7 | async-start | bytes 3538944
  469.1 51.1 %collective-permute-start.10 = (bf16[384,6144]{1,0:T(8,128)(2,1)}, bf16[384,6144]{1,0:T(8,128)(2,1)}, u32[]{:S(2)}, u32[]{:S(2)}) collective-permute-start(bf16[384,6144]{1,0:T(8,128)(2,1)} %split.163), channel_id=1, source_target_pairs={{0,8},{1,9},{2,10},{3,11},{4,12},{5,13},{6,14},{7,15},{8,0},{9,1},... | collective-permute-start | bytes 14155784 | tf_op jit(solution)/shard_map/ppermute | solution.py:40
  514.5 29.5 %collective-permute-start.21 = (bf16[384,1536]{1,0:T(8,128)(2,1)}, bf16[384,1536]{1,0:T(8,128)(2,1)}, u32[]{:S(2)}, u32[]{:S(2)}) collective-permute-start(bf16[384,1536]{1,0:T(8,128)(2,1)} %get-tuple-element.233), channel_id=1, source_target_pairs={{0,32},{1,33},{2,34},{3,35},{4,36},{5,37},{6,38},{7,39},{8,40},{9,... | collective-permute-start | bytes 3538952 | tf_op jit(solution)/shard_map/ppermute | solution.py:40
  516.0 48.6 %collective-permute-start.22 = (bf16[384,1536]{1,0:T(8,128)(2,1)}, bf16[384,1536]{1,0:T(8,128)(2,1)}, u32[]{:S(2)}, u32[]{:S(2)}) collective-permute-start(bf16[384,1536]{1,0:T(8,128)(2,1)} %get-tuple-element.235), channel_id=1, source_target_pairs={{0,64},{1,65},{2,66},{3,67},{4,68},{5,69},{6,70},{7,71},{8,72},{9,... | collective-permute-start | bytes 3538952 | tf_op jit(solution)/shard_map/ppermute | solution.py:40
  518.8 45.9 %collective-permute-start.23 = (bf16[384,1536]{1,0:T(8,128)(2,1)}, bf16[384,1536]{1,0:T(8,128)(2,1)}, u32[]{:S(2)}, u32[]{:S(2)}) collective-permute-start(bf16[384,1536]{1,0:T(8,128)(2,1)} %get-tuple-element.234), channel_id=1, source_target_pairs={{0,96},{1,97},{2,98},{3,99},{4,100},{5,101},{6,102},{7,103},{8,104... | collective-permute-start | bytes 3538952 | tf_op jit(solution)/shard_map/ppermute | solution.py:40
  524.8 68.7 %collective-permute-start.11 = (bf16[96,6144]{1,0:T(8,128)(2,1)S(1)}, bf16[96,6144]{1,0:T(8,128)(2,1)S(1)}, u32[]{:S(2)}, u32[]{:S(2)}) collective-permute-start(bf16[96,6144]{1,0:T(8,128)(2,1)S(1)} %get-tuple-element.236), channel_id=1, source_target_pairs={{0,1},{1,2},{2,3},{3,0},{4,5},{5,6},{6,7},{7,4},{8,9},{9,10},{10,1... | collective-permute-start | bytes 3538952 | tf_op jit(solution)/shard_map/ppermute | solution.py:40
  524.9 69.6 %collective-permute-start.12 = (bf16[96,6144]{1,0:T(8,128)(2,1)S(1)}, bf16[96,6144]{1,0:T(8,128)(2,1)S(1)}, u32[]{:S(2)}, u32[]{:S(2)}) collective-permute-start(bf16[96,6144]{1,0:T(8,128)(2,1)S(1)} %get-tuple-element.238), channel_id=1, source_target_pairs={{0,2},{1,3},{2,0},{3,1},{4,6},{5,7},{6,4},{7,5},{8,10},{9,11},{10,... | collective-permute-start | bytes 3538952 | tf_op jit(solution)/shard_map/ppermute | solution.py:40
  544.0 51.8 %collective-permute-start.13 = (bf16[96,6144]{1,0:T(8,128)(2,1)S(1)}, bf16[96,6144]{1,0:T(8,128)(2,1)S(1)}, u32[]{:S(2)}, u32[]{:S(2)}) collective-permute-start(bf16[96,6144]{1,0:T(8,128)(2,1)S(1)} %get-tuple-element.237), channel_id=1, source_target_pairs={{0,3},{1,0},{2,1},{3,2},{4,7},{5,4},{6,5},{7,6},{8,11},{9,8},{10,9... | collective-permute-start | bytes 3538952 | tf_op jit(solution)/shard_map/ppermute | solution.py:40
  568.2 85.6 %collective-permute-start.24 = (bf16[96,1536]{1,0:T(8,128)(2,1)}, bf16[96,1536]{1,0:T(8,128)(2,1)}, u32[]{:S(2)}, u32[]{:S(2)}) collective-permute-start(bf16[96,1536]{1,0:T(8,128)(2,1)} %get-tuple-element.246), channel_id=1, source_target_pairs={{0,1},{1,2},{2,3},{3,0},{4,5},{5,6},{6,7},{7,4},{8,9},{9,10},{10,1... | collective-permute-start | bytes 884744 | tf_op jit(solution)/shard_map/ppermute | solution.py:40
  568.2 89.0 %collective-permute-start.25 = (bf16[96,1536]{1,0:T(8,128)(2,1)}, bf16[96,1536]{1,0:T(8,128)(2,1)}, u32[]{:S(2)}, u32[]{:S(2)}) collective-permute-start(bf16[96,1536]{1,0:T(8,128)(2,1)} %get-tuple-element.248), channel_id=1, source_target_pairs={{0,2},{1,3},{2,0},{3,1},{4,6},{5,7},{6,4},{7,5},{8,10},{9,11},{10,... | collective-permute-start | bytes 884744 | tf_op jit(solution)/shard_map/ppermute | solution.py:40
  597.5 52.3 %collective-permute-start.14 = (bf16[24,6144]{1,0:T(8,128)(2,1)}, bf16[24,6144]{1,0:T(8,128)(2,1)}, u32[]{:S(2)}, u32[]{:S(2)}) collective-permute-start(bf16[24,6144]{1,0:T(8,128)(2,1)} %get-tuple-element.249), channel_id=1, source_target_pairs={{0,4},{1,5},{2,6},{3,7},{4,16},{5,17},{6,18},{7,19},{8,12},{9,13},... | collective-permute-start | bytes 884744 | tf_op jit(solution)/shard_map/ppermute | solution.py:40
  598.5 51.9 %collective-permute-start.15 = (bf16[24,6144]{1,0:T(8,128)(2,1)}, bf16[24,6144]{1,0:T(8,128)(2,1)}, u32[]{:S(2)}, u32[]{:S(2)}) collective-permute-start(bf16[24,6144]{1,0:T(8,128)(2,1)} %get-tuple-element.251), channel_id=1, source_target_pairs={{0,16},{1,17},{2,18},{3,19},{4,20},{5,21},{6,22},{7,23},{8,24},{9,... | collective-permute-start | bytes 884744 | tf_op jit(solution)/shard_map/ppermute | solution.py:40
  601.3 49.3 %collective-permute-start.16 = (bf16[24,6144]{1,0:T(8,128)(2,1)}, bf16[24,6144]{1,0:T(8,128)(2,1)}, u32[]{:S(2)}, u32[]{:S(2)}) collective-permute-start(bf16[24,6144]{1,0:T(8,128)(2,1)} %get-tuple-element.250), channel_id=1, source_target_pairs={{0,20},{1,21},{2,22},{3,23},{4,0},{5,1},{6,2},{7,3},{8,28},{9,29},... | collective-permute-start | bytes 884744 | tf_op jit(solution)/shard_map/ppermute | solution.py:40
  666.5 57.5 %collective-permute-start.1 = (bf16[96,6272]{1,0:T(8,128)(2,1)S(1)}, bf16[96,6272]{1,0:T(8,128)(2,1)S(1)}, u32[]{:S(2)}, u32[]{:S(2)}) collective-permute-start(bf16[96,6272]{1,0:T(8,128)(2,1)S(1)} %bitcast.406), channel_id=1, source_target_pairs={{0,4},{1,5},{2,6},{3,7},{4,16},{5,17},{6,18},{7,19},{8,12},{9,13},... | collective-permute-start | bytes 3612680 | tf_op jit(solution)/shard_map/ppermute | solution.py:40
  668.2 55.7 %collective-permute-start.2 = (bf16[96,6272]{1,0:T(8,128)(2,1)S(1)}, bf16[96,6272]{1,0:T(8,128)(2,1)S(1)}, u32[]{:S(2)}, u32[]{:S(2)}) collective-permute-start(bf16[96,6272]{1,0:T(8,128)(2,1)S(1)} %bitcast.405), channel_id=1, source_target_pairs={{0,16},{1,17},{2,18},{3,19},{4,20},{5,21},{6,22},{7,23},{8,24},{9,... | collective-permute-start | bytes 3612680 | tf_op jit(solution)/shard_map/ppermute | solution.py:40
  668.8 55.1 %collective-permute-start.3 = (bf16[96,6272]{1,0:T(8,128)(2,1)S(1)}, bf16[96,6272]{1,0:T(8,128)(2,1)S(1)}, u32[]{:S(2)}, u32[]{:S(2)}) collective-permute-start(bf16[96,6272]{1,0:T(8,128)(2,1)S(1)} %bitcast.404), channel_id=1, source_target_pairs={{0,20},{1,21},{2,22},{3,23},{4,0},{5,1},{6,2},{7,3},{8,28},{9,29},... | collective-permute-start | bytes 3612680 | tf_op jit(solution)/shard_map/ppermute | solution.py:40
  671.0 52.9 %collective-permute-start.29 = (bf16[24,1536]{1,0:T(8,128)(2,1)S(1)}, bf16[24,1536]{1,0:T(8,128)(2,1)S(1)}, u32[]{:S(2)}, u32[]{:S(2)}) collective-permute-start(bf16[24,1536]{1,0:T(8,128)(2,1)S(1)} %get-tuple-element.256), channel_id=1, source_target_pairs={{0,20},{1,21},{2,22},{3,23},{4,0},{5,1},{6,2},{7,3},{8,28},{9,29},... | collective-permute-start | bytes 221192 | tf_op jit(solution)/shard_map/ppermute | solution.py:40
  724.7 15.7 %collective-permute-start.4 = (bf16[24,6272]{1,0:T(8,128)(2,1)S(1)}, bf16[24,6272]{1,0:T(8,128)(2,1)S(1)}, u32[]{:S(2)}, u32[]{:S(2)}) collective-permute-start(bf16[24,6272]{1,0:T(8,128)(2,1)S(1)} %get-tuple-element.243), channel_id=1, source_target_pairs={{0,1},{1,2},{2,3},{3,0},{4,5},{5,6},{6,7},{7,4},{8,9},{9,10},{10,1... | collective-permute-start | bytes 903176 | tf_op jit(solution)/shard_map/ppermute | solution.py:40
  (199 other events, 2008.5 us)
Sparse Core Ops, SparseCore 0:
  17.0 46.8 all-gather.2
  109.3 43.9 all-gather.4
  226.3 74.1 all-reduce.7
  302.9 45.3 reduce-scatter.6
  423.5 74.6 all-reduce.9
  500.4 69.8 reduce-scatter.8
